TPU v7x, 512 devices: a whole 4x8x8 slice. The times are simulated.
512 devices in a mesh: dp: 32 (over y, x_hi, core), tensor: 16 (over x_lo, z).
Axes of the slice: x: 4 (x_hi: 2, x_lo: 2; x = x_hi * 2 + x_lo), y: 8, z: 8, core: 2. Of those that a mesh axis runs over, the one named last changes fastest.
Arguments:
- attn: bfloat16 [4096, 4096], P('dp', 'tensor'), may hold values from -6 to 6
- residual: bfloat16 [4096, 4096], P('dp', 'tensor'), may hold values from -6 to 6
- o_weight: bfloat16 [4096, 4096], P('tensor'), may hold values from -0.09375 to 0.09375
- encoder: bfloat16 [4096, 1024], P(('dp', 'tensor')), may hold values from -0.09375 to 0.09375
- decoder: bfloat16 [1024, 4096], P(None, 'tensor'), may hold values from -0.1875 to 0.1875
- grad_out: bfloat16 [4096, 4096], P('dp', 'tensor'), may hold values from -6 to 6
Outputs:
- output: bfloat16 [4096, 4096], P('dp', 'tensor')
- grad_attn: bfloat16 [4096, 4096], P('dp', 'tensor')
- grad_weight: float32 [4096, 4096], P('tensor', 'dp')
All inputs are finite; a program needn't handle non-finite values.
Results may differ from a plain program's by a relative error of at most 0.0095.
Values may be sent and summed in bfloat16 or wider, within the bound.
No kernel may reach another device: no remote copies, remote signals or barrier semaphores. Data moves between devices by JAX's collectives and lax.ppermute only.
A program may use at most 64 MiB of HBM per device.

v0:
```python
import jax
import jax.numpy as jnp
from jax import lax
from jax.sharding import Mesh, PartitionSpec as P

SIZES = (8, 2, 2, 2, 8)
NAMES = ("y", "xh", "core", "xl", "z")
DP = ("y", "xh", "core")
CHIPS = ("y", "xh")
TENSOR = ("xl", "z")
SWAP = [(0, 1), (1, 0)]
F32, BF16 = jnp.float32, jnp.bfloat16


def dot(a, b, contract):
    return lax.dot_general(a, b, ((contract[:1], contract[1:]), ((), ())), preferred_element_type=F32)


def exchange(blocks, axes):
    return lax.all_to_all(blocks, axes, 0, 0)


def spread(block, n):
    return jnp.broadcast_to(block[None], (n,) + block.shape)


def total(blocks):
    return jnp.sum(blocks.astype(F32), axis=0).astype(BF16)


def together(*arrays):
    return lax.optimization_barrier(arrays)


def swap(x):
    return lax.ppermute(x, "core", SWAP)


def pair_rows(mine, mate):
    return jnp.concatenate([mine.astype(BF16).reshape(16, 8, -1), mate.astype(BF16).reshape(16, 8, -1)], 1)


def per_device(attn, residual, o_weight, encoder, decoder, grad_out):
    core = lax.axis_index("core")
    block = lax.axis_index(DP)
    starts = [x.astype(jnp.uint32) for x in (block * 128, (block + 1 - 2 * core) * 128, core * 512, 512 - core * 512)]

    def part(x, start, size, axis):
        return lax.dynamic_slice_in_dim(x, start, size, axis)

    back_term = dot(grad_out, decoder, (1, 1)).astype(BF16)
    enc_mine, enc_sent = part(encoder, starts[2], 512, 1), part(encoder, starts[3], 512, 1)
    got, attn_mate, enc_mine, enc_sent, core_is_0, *starts = together(
        exchange(back_term.reshape(16, 8, 1024), TENSOR), swap(attn), enc_mine, enc_sent, core == 0, *starts
    )
    rows = total(got)
    came = swap(jnp.concatenate([part(rows, starts[3], 512, 1), enc_sent], 0))
    rows = jnp.concatenate([part(rows, starts[2], 512, 1), enc_mine, came], 0)
    got = exchange(spread(rows, 16), TENSOR)
    back, enc, back_mate, enc_mate = [got[:, i : i + 8].reshape(128, 512) for i in (0, 8, 16, 24)]

    fold_term = dot(part(o_weight, starts[0], 128, 1), enc, (1, 0)) + dot(part(o_weight, starts[1], 128, 1), enc_mate, (1, 0))
    gram_term = dot(attn, back, (0, 0)) + dot(attn_mate, back_mate, (0, 0))
    got = exchange(
        jnp.concatenate([fold_term.astype(BF16), gram_term.astype(BF16)], 1).reshape(16, 16, 1024), CHIPS
    )
    got = exchange(spread(total(got), 16), CHIPS).reshape(256, 1024)
    fold, gram = got[:, :512], got[:, 512:]

    code = pair_rows(dot(attn, fold, (1, 0)), dot(attn_mate, fold, (1, 0)))
    code, fold, gram = together(code, fold, gram)
    rows = total(exchange(code, TENSOR))
    mine, came = rows[:8], swap(rows[8:])
    rows = jnp.where(core_is_0, jnp.concatenate([mine, came], 1), jnp.concatenate([came, mine], 1))
    total_code = exchange(spread(rows, 16), TENSOR).reshape(128, 1024)
    mixed = dot(total_code, decoder, (1, 0))
    output = (residual.astype(F32) + mixed).astype(BF16)

    attn_term = dot(back_mate, fold, (1, 1))
    terms = swap(jnp.concatenate([dot(gram, enc_mate, (1, 1)), attn_term[:, :128], attn_term[:, 128:]], 0))
    grad_weight = dot(gram, enc, (1, 1)) + terms[:256]
    grad_attn = dot(back, fold, (1, 1)) + jnp.concatenate([terms[256:384], terms[384:]], 1)
    return output, grad_attn.astype(BF16), grad_weight


def solution(mesh):
    fine = Mesh(mesh.devices.reshape(SIZES), NAMES)
    return jax.shard_map(
        per_device,
        mesh=fine,
        in_specs=(
            P(DP, TENSOR),
            P(DP, TENSOR),
            P(TENSOR, None),
            P(DP + TENSOR, None),
            P(None, TENSOR),
            P(DP, TENSOR),
        ),
        out_specs=(P(DP, TENSOR), P(DP, TENSOR), P(TENSOR, DP)),
        check_vma=False,
    )
```

profile of v0, /device:TPU:2, one launch (start us, length us, event | category | flops | bytes accessed | tf_op | source)
XLA Modules:
  0.0 133.6 jit_solution(17146905479513616490)
XLA Ops:
  0.6 0.0 copy-start
  0.6 0.0 copy-start.1
  0.7 2.3 %fusion.2 = bf16[16,8,1024]{2,1,0:T(8,128)(2,1)} fusion(bf16[128,256]{1,0:T(8,128)(2,1)} %param.11, bf16[1024,256]{1,0:T(8,128)(2,1)} %param.10), kind=kOutput, calls=%fused_computation.6 | convolution fusion | flops 67239936 | bytes 851968 | tf_op jit(solution)/shard_map/dot_general | solution.py:16
  2.9 11.8 %all-to-all-start = ((bf16[16,8,1024]{2,1,0:T(8,128)(2,1)}), bf16[16,8,1024]{2,1,0:T(8,128)(2,1)S(1)}, u32[]{:S(2)}, u32[]{:S(2)}) async-start(bf16[16,8,1024]{2,1,0:T(8,128)(2,1)} %fusion.2), calls=%async_computation | async-start | bytes 524288 | tf_op jit(solution)/shard_map/all_to_all | solution.py:20
  14.7 1.9 %collective-permute-start = (bf16[128,256]{1,0:T(8,128)(2,1)}, bf16[128,256]{1,0:T(8,128)(2,1)S(1)}, u32[]{:S(2)}, u32[]{:S(2)}) collective-permute-start(bf16[128,256]{1,0:T(8,128)(2,1)} %param.6), channel_id=1, source_target_pairs={{0,16},{16,0},{1,17},{17,1},{2,18},{18,2},{3,19},{19,3},{4,20},{20... | collective-permute-start | bytes 196616 | tf_op jit(solution)/shard_map/ppermute | solution.py:36
  16.6 0.9 constant_dynamic-slice_fusion.2
  17.5 0.6 collective-permute-done
  18.1 6.1 %all-to-all-done = bf16[16,8,1024]{2,1,0:T(8,128)(2,1)S(1)} async-done(((bf16[16,8,1024]{2,1,0:T(8,128)(2,1)}), bf16[16,8,1024]{2,1,0:T(8,128)(2,1)S(1)}, u32[]{:S(2)}, u32[]{:S(2)}) %all-to-all-start) | async-done | bytes 262176 | tf_op jit(solution)/shard_map/all_to_all | solution.py:20
  24.2 0.1 constant_dynamic-slice_fusion.1
  24.3 1.9 %collective-permute-start.1 = (bf16[16,512]{1,0:T(8,128)(2,1)S(1)}, bf16[16,512]{1,0:T(8,128)(2,1)S(1)}, u32[]{:S(2)}, u32[]{:S(2)}) collective-permute-start(bf16[16,512]{1,0:T(8,128)(2,1)S(1)} %pad_maximum_fusion.4), channel_id=1, source_target_pairs={{0,16},{16,0},{1,17},{17,1},{2,18},{18,2},{3,19},{19,3},{4,20},{20... | collective-permute-start | bytes 49160 | tf_op jit(solution)/shard_map/ppermute | solution.py:36
  26.2 1.1 collective-permute-done.1
  27.4 19.9 %all_to_all.30 = bf16[16,32,512]{2,1,0:T(8,128)(2,1)S(1)} all-to-all(bf16[16,32,512]{2,1,0:T(8,128)(2,1)S(1)} %broadcast_in_dim.6), channel_id=1, replica_groups=mesh['y'=8,'xh'=2,'core'=2,'xl'=2,'z'=8] {'xl','z'}, dimensions={0} | all-to-all | bytes 1048576 | tf_op jit(solution)/shard_map/all_to_all | solution.py:20
  47.3 0.0 copy-done.1
  47.3 0.3 convolution_bitcast_fusion
  47.6 0.2 fusion.1
  47.8 0.0 copy-done
  47.9 0.3 fusion.10
  48.1 0.3 fusion
  48.4 0.1 pad_maximum_fusion
  48.5 24.6 %all_to_all.31 = bf16[16,16,1024]{2,1,0:T(8,128)(2,1)S(1)} all-to-all(bf16[16,16,1024]{2,1,0:T(8,128)(2,1)S(1)} %bitcast.49), channel_id=1, replica_groups=mesh['y'=8,'xh'=2,'core'=2,'xl'=2,'z'=8] {'y','xh'}, dimensions={0} | all-to-all | bytes 1048576 | tf_op jit(solution)/shard_map/all_to_all | solution.py:20
  73.1 0.1 reduce_sum.37
  73.1 0.1 broadcast_in_dim.7
  73.2 18.7 %all_to_all.32 = bf16[16,16,1024]{2,1,0:T(8,128)(2,1)S(1)} all-to-all(bf16[16,16,1024]{2,1,0:T(8,128)(2,1)S(1)} %broadcast_in_dim.7), channel_id=1, replica_groups=mesh['y'=8,'xh'=2,'core'=2,'xl'=2,'z'=8] {'y','xh'}, dimensions={0} | all-to-all | bytes 1048576 | tf_op jit(solution)/shard_map/all_to_all | solution.py:20
  91.9 0.2 fusion.3
  92.1 0.2 fusion.4
  92.3 0.7 pad_maximum_fusion.1
  93.1 11.8 %all-to-all-start.4 = ((bf16[16,16,512]{2,1,0:T(8,128)(2,1)}), bf16[16,16,512]{2,1,0:T(8,128)(2,1)S(1)}, u32[]{:S(2)}, u32[]{:S(2)}) async-start(bf16[16,16,512]{2,1,0:T(8,128)(2,1)} %pad_maximum_fusion.1), calls=%async_computation.4 | async-start | bytes 524288 | tf_op jit(solution)/shard_map/all_to_all | solution.py:20
  104.9 0.2 fusion.12
  105.1 0.0 copy-start.2
  105.2 0.2 fusion.9
  105.4 0.7 pad_maximum_fusion.2
  106.1 1.9 %collective-permute-start.3 = (f32[512,128]{1,0:T(8,128)}, f32[512,128]{1,0:T(8,128)}, u32[]{:S(2)}, u32[]{:S(2)}) collective-permute-start(f32[512,128]{1,0:T(8,128)} %pad_maximum_fusion.2), channel_id=1, source_target_pairs={{0,16},{16,0},{1,17},{17,1},{2,18},{18,2},{3,19},{19,3},{4,20},{20... | collective-permute-start | bytes 786440 | tf_op jit(solution)/shard_map/ppermute | solution.py:36
  108.0 5.0 %all-to-all-done.4 = bf16[16,16,512]{2,1,0:T(8,128)(2,1)S(1)} async-done(((bf16[16,16,512]{2,1,0:T(8,128)(2,1)}), bf16[16,16,512]{2,1,0:T(8,128)(2,1)S(1)}, u32[]{:S(2)}, u32[]{:S(2)}) %all-to-all-start.4) | async-done | bytes 262176 | tf_op jit(solution)/shard_map/all_to_all | solution.py:20
  113.0 1.9 %collective-permute-start.2 = (bf16[8,512]{1,0:T(8,128)(2,1)S(1)}, bf16[8,512]{1,0:T(8,128)(2,1)S(1)}, u32[]{:S(2)}, u32[]{:S(2)}) collective-permute-start(bf16[8,512]{1,0:T(8,128)(2,1)S(1)} %get-tuple-element.34), channel_id=1, source_target_pairs={{0,16},{16,0},{1,17},{17,1},{2,18},{18,2},{3,19},{19,3},{4,20},{20... | collective-permute-start | bytes 24584 | tf_op jit(solution)/shard_map/ppermute | solution.py:36
  115.0 1.1 collective-permute-done.2
  116.1 0.7 broadcast_in_dim.8
  116.8 5.2 %all-to-all-start.5 = ((bf16[16,8,1024]{2,1,0:T(8,128)(2,1)}), bf16[16,8,1024]{2,1,0:T(8,128)(2,1)S(1)}, u32[]{:S(2)}, u32[]{:S(2)}) async-start(bf16[16,8,1024]{2,1,0:T(8,128)(2,1)} %broadcast_in_dim.8), calls=%async_computation.5 | async-start | bytes 524288 | tf_op jit(solution)/shard_map/all_to_all | solution.py:20
  122.0 0.0 collective-permute-done.3
  122.0 0.9 fusion.20
  122.9 0.9 fusion.7
  123.7 1.8 %slice_add_fusion = f32[256,128]{1,0:T(8,128)} fusion(f32[512,128]{1,0:T(8,128)} %collective-permute-done.3, bf16[256,512]{1,0:T(8,128)(2,1)S(1)} %get-tuple-element.26, bf16[16,32,512]{2,1,0:T(8,128)(2,1)S(1)} %all_to_all.30), kind=kOutput, calls=%fused_computation.17 | convolution fusion | flops 33587200 | bytes 655360 | tf_op jit(solution)/shard_map/dot_general | solution.py:16
  125.5 6.2 %all-to-all-done.5 = bf16[16,8,1024]{2,1,0:T(8,128)(2,1)S(1)} async-done(((bf16[16,8,1024]{2,1,0:T(8,128)(2,1)}), bf16[16,8,1024]{2,1,0:T(8,128)(2,1)S(1)}, u32[]{:S(2)}, u32[]{:S(2)}) %all-to-all-start.5) | async-done | bytes 262176 | tf_op jit(solution)/shard_map/all_to_all | solution.py:20
  131.7 0.0 copy-done.2
  131.7 1.9 %fusion.5 = bf16[128,256]{1,0:T(8,128)(2,1)} fusion(bf16[1024,256]{1,0:T(8,128)(2,1)} %param.10, bf16[16,8,1024]{2,1,0:T(8,128)(2,1)S(1)} %all-to-all-done.5, bf16[128,256]{1,0:T(8,128)(2,1)S(1)} %copy-done.2), kind=kOutput, calls=%fused_computation.12 | convolution fusion | flops 67207168 | bytes 917504 | tf_op jit(solution)/shard_map/dot_general | solution.py:16
  (9 shorter events, 0.2 us)
Async XLA Ops:
  0.6 47.2 %copy-start = (bf16[256,4096]{1,0:T(8,128)(2,1)S(1)}, bf16[256,4096]{1,0:T(8,128)(2,1)}, u32[]{:S(2)}) copy-start(bf16[256,4096]{1,0:T(8,128)(2,1)} %param.8) | copy-start | bytes 6291460
  0.6 46.7 %copy-start.1 = (bf16[128,256]{1,0:T(8,128)(2,1)S(1)}, bf16[128,256]{1,0:T(8,128)(2,1)}, u32[]{:S(2)}) copy-start(bf16[128,256]{1,0:T(8,128)(2,1)} %param.6) | copy-start | bytes 196612
  2.9 21.2 %all-to-all-start = ((bf16[16,8,1024]{2,1,0:T(8,128)(2,1)}), bf16[16,8,1024]{2,1,0:T(8,128)(2,1)S(1)}, u32[]{:S(2)}, u32[]{:S(2)}) async-start(bf16[16,8,1024]{2,1,0:T(8,128)(2,1)} %fusion.2), calls=%async_computation | async-start | bytes 524288 | tf_op jit(solution)/shard_map/all_to_all | solution.py:20
  14.7 3.3 %collective-permute-start = (bf16[128,256]{1,0:T(8,128)(2,1)}, bf16[128,256]{1,0:T(8,128)(2,1)S(1)}, u32[]{:S(2)}, u32[]{:S(2)}) collective-permute-start(bf16[128,256]{1,0:T(8,128)(2,1)} %param.6), channel_id=1, source_target_pairs={{0,16},{16,0},{1,17},{17,1},{2,18},{18,2},{3,19},{19,3},{4,20},{20... | collective-permute-start | bytes 196616 | tf_op jit(solution)/shard_map/ppermute | solution.py:36
  24.3 3.1 %collective-permute-start.1 = (bf16[16,512]{1,0:T(8,128)(2,1)S(1)}, bf16[16,512]{1,0:T(8,128)(2,1)S(1)}, u32[]{:S(2)}, u32[]{:S(2)}) collective-permute-start(bf16[16,512]{1,0:T(8,128)(2,1)S(1)} %pad_maximum_fusion.4), channel_id=1, source_target_pairs={{0,16},{16,0},{1,17},{17,1},{2,18},{18,2},{3,19},{19,3},{4,20},{20... | collective-permute-start | bytes 49160 | tf_op jit(solution)/shard_map/ppermute | solution.py:36
  93.1 19.9 %all-to-all-start.4 = ((bf16[16,16,512]{2,1,0:T(8,128)(2,1)}), bf16[16,16,512]{2,1,0:T(8,128)(2,1)S(1)}, u32[]{:S(2)}, u32[]{:S(2)}) async-start(bf16[16,16,512]{2,1,0:T(8,128)(2,1)} %pad_maximum_fusion.1), calls=%async_computation.4 | async-start | bytes 524288 | tf_op jit(solution)/shard_map/all_to_all | solution.py:20
  105.1 26.6 %copy-start.2 = (bf16[128,256]{1,0:T(8,128)(2,1)S(1)}, bf16[128,256]{1,0:T(8,128)(2,1)}, u32[]{:S(2)}) copy-start(bf16[128,256]{1,0:T(8,128)(2,1)} %param.7) | copy-start | bytes 196612
  106.1 15.9 %collective-permute-start.3 = (f32[512,128]{1,0:T(8,128)}, f32[512,128]{1,0:T(8,128)}, u32[]{:S(2)}, u32[]{:S(2)}) collective-permute-start(f32[512,128]{1,0:T(8,128)} %pad_maximum_fusion.2), channel_id=1, source_target_pairs={{0,16},{16,0},{1,17},{17,1},{2,18},{18,2},{3,19},{19,3},{4,20},{20... | collective-permute-start | bytes 786440 | tf_op jit(solution)/shard_map/ppermute | solution.py:36
  113.0 3.1 %collective-permute-start.2 = (bf16[8,512]{1,0:T(8,128)(2,1)S(1)}, bf16[8,512]{1,0:T(8,128)(2,1)S(1)}, u32[]{:S(2)}, u32[]{:S(2)}) collective-permute-start(bf16[8,512]{1,0:T(8,128)(2,1)S(1)} %get-tuple-element.34), channel_id=1, source_target_pairs={{0,16},{16,0},{1,17},{17,1},{2,18},{18,2},{3,19},{19,3},{4,20},{20... | collective-permute-start | bytes 24584 | tf_op jit(solution)/shard_map/ppermute | solution.py:36
  116.8 14.9 %all-to-all-start.5 = ((bf16[16,8,1024]{2,1,0:T(8,128)(2,1)}), bf16[16,8,1024]{2,1,0:T(8,128)(2,1)S(1)}, u32[]{:S(2)}, u32[]{:S(2)}) async-start(bf16[16,8,1024]{2,1,0:T(8,128)(2,1)} %broadcast_in_dim.8), calls=%async_computation.5 | async-start | bytes 524288 | tf_op jit(solution)/shard_map/all_to_all | solution.py:20
where the time goes:
time: 135 us; the launch traced here: 134 us
  blocking collectives  63.2 us (47%)
  starting transfers between devices  36.4 us (27%)
  waiting for transfers between devices  20.1 us (15%)
  matrix products  8.68 us (6%)
  local copies, waits for them, and re-layouts  2.73 us (2%)
  other arithmetic  1.69 us (1%)
    all_to_all x3, blocking collectives, exchange(): return lax.all_to_all(blocks, axes, 0, 0)  63.2 us
    all_to_all x3, starting transfers between devices, exchange(): return lax.all_to_all(blocks, axes, 0, 0)  28.8 us
    all_to_all x3, waiting for transfers between devices, exchange(): return lax.all_to_all(blocks, axes, 0, 0)  17.2 us
    dot_general x12, matrix products, dot(): lax.dot_general(a, b, ((contract[:1], contract[1:]), ((), ())), preferred...  8.68 us
    ppermute x4, starting transfers between devices, swap(): return lax.ppermute(x, 'core', SWAP)  7.65 us
    ppermute x4, waiting for transfers between devices, swap(): return lax.ppermute(x, 'core', SWAP)  2.84 us
  transfers between devices with their start and end apart: 7, of which 6 were waited for; matrix products, arithmetic and copies ran while one was open for 5% of the time, Pallas kernels for 0%

commit v1 on v0

--- a/solution.py
+++ b/solution.py
@@ -6,7 +6,7 @@
 SIZES = (8, 2, 2, 2, 8)
 NAMES = ("y", "xh", "core", "xl", "z")
 DP = ("y", "xh", "core")
-CHIPS = ("y", "xh")
+CHIPS = ("xh", "y")
 TENSOR = ("xl", "z")
 SWAP = [(0, 1), (1, 0)]
 F32, BF16 = jnp.float32, jnp.bfloat16

time: 135 us -> 132 us (0.978)
  the two profiles are of different devices: /device:TPU:2 before, /device:TPU:8 now
where the time goes in v1:
time: 132 us; the launch traced here: 131 us
  blocking collectives  63.9 us (48%)
  starting transfers between devices  30.9 us (23%)
  waiting for transfers between devices  22.4 us (17%)
  matrix products  8.69 us (7%)
  local copies, waits for them, and re-layouts  2.73 us (2%)
  other arithmetic  1.69 us (1%)
    all_to_all x3, blocking collectives, exchange(): return lax.all_to_all(blocks, axes, 0, 0)  63.9 us
    all_to_all x3, starting transfers between devices, exchange(): return lax.all_to_all(blocks, axes, 0, 0)  23.2 us
    all_to_all x3, waiting for transfers between devices, exchange(): return lax.all_to_all(blocks, axes, 0, 0)  19.6 us
    dot_general x12, matrix products, dot(): lax.dot_general(a, b, ((contract[:1], contract[1:]), ((), ())), preferred...  8.69 us
    ppermute x4, starting transfers between devices, swap(): return lax.ppermute(x, 'core', SWAP)  7.67 us
    ppermute x4, waiting for transfers between devices, swap(): return lax.ppermute(x, 'core', SWAP)  2.84 us
  transfers between devices with their start and end apart: 7, of which 6 were waited for; matrix products, arithmetic and copies ran while one was open for 5% of the time, Pallas kernels for 0%

profile of v1, /device:TPU:8, one launch (start us, length us, event | category | flops | bytes accessed | tf_op | source)
XLA Modules:
  0.0 131.2 jit_solution(15097255565727411128)
XLA Ops:
  0.6 0.0 copy-start
  0.6 0.0 copy-start.1
  0.7 2.3 %fusion.2 = bf16[16,8,1024]{2,1,0:T(8,128)(2,1)} fusion(bf16[128,256]{1,0:T(8,128)(2,1)} %param.11, bf16[1024,256]{1,0:T(8,128)(2,1)} %param.10), kind=kOutput, calls=%fused_computation.6 | convolution fusion | flops 67239936 | bytes 851968 | tf_op jit(solution)/shard_map/dot_general | solution.py:16
  2.9 11.4 %all-to-all-start = ((bf16[16,8,1024]{2,1,0:T(8,128)(2,1)}), bf16[16,8,1024]{2,1,0:T(8,128)(2,1)S(1)}, u32[]{:S(2)}, u32[]{:S(2)}) async-start(bf16[16,8,1024]{2,1,0:T(8,128)(2,1)} %fusion.2), calls=%async_computation | async-start | bytes 524288 | tf_op jit(solution)/shard_map/all_to_all | solution.py:20
  14.3 1.9 %collective-permute-start = (bf16[128,256]{1,0:T(8,128)(2,1)}, bf16[128,256]{1,0:T(8,128)(2,1)S(1)}, u32[]{:S(2)}, u32[]{:S(2)}) collective-permute-start(bf16[128,256]{1,0:T(8,128)(2,1)} %param.6), channel_id=1, source_target_pairs={{0,16},{16,0},{1,17},{17,1},{2,18},{18,2},{3,19},{19,3},{4,20},{20... | collective-permute-start | bytes 196616 | tf_op jit(solution)/shard_map/ppermute | solution.py:36
  16.2 0.9 constant_dynamic-slice_fusion.2
  17.1 0.6 collective-permute-done
  17.6 6.7 %all-to-all-done = bf16[16,8,1024]{2,1,0:T(8,128)(2,1)S(1)} async-done(((bf16[16,8,1024]{2,1,0:T(8,128)(2,1)}), bf16[16,8,1024]{2,1,0:T(8,128)(2,1)S(1)}, u32[]{:S(2)}, u32[]{:S(2)}) %all-to-all-start) | async-done | bytes 262176 | tf_op jit(solution)/shard_map/all_to_all | solution.py:20
  24.4 0.1 constant_dynamic-slice_fusion.1
  24.5 1.9 %collective-permute-start.1 = (bf16[16,512]{1,0:T(8,128)(2,1)S(1)}, bf16[16,512]{1,0:T(8,128)(2,1)S(1)}, u32[]{:S(2)}, u32[]{:S(2)}) collective-permute-start(bf16[16,512]{1,0:T(8,128)(2,1)S(1)} %pad_maximum_fusion.4), channel_id=1, source_target_pairs={{0,16},{16,0},{1,17},{17,1},{2,18},{18,2},{3,19},{19,3},{4,20},{20... | collective-permute-start | bytes 49160 | tf_op jit(solution)/shard_map/ppermute | solution.py:36
  26.5 1.1 collective-permute-done.1
  27.7 20.1 %all_to_all.30 = bf16[16,32,512]{2,1,0:T(8,128)(2,1)S(1)} all-to-all(bf16[16,32,512]{2,1,0:T(8,128)(2,1)S(1)} %broadcast_in_dim.6), channel_id=1, replica_groups=mesh['y'=8,'xh'=2,'core'=2,'xl'=2,'z'=8] {'xl','z'}, dimensions={0} | all-to-all | bytes 1048576 | tf_op jit(solution)/shard_map/all_to_all | solution.py:20
  47.7 0.0 copy-done.1
  47.8 0.3 convolution_bitcast_fusion
  48.0 0.2 fusion.1
  48.3 0.0 copy-done
  48.3 0.3 fusion.10
  48.6 0.3 fusion
  48.9 0.1 pad_maximum_fusion
  48.9 24.0 %all_to_all.31 = bf16[16,16,1024]{2,1,0:T(8,128)(2,1)S(1)} all-to-all(bf16[16,16,1024]{2,1,0:T(8,128)(2,1)S(1)} %bitcast.49), channel_id=1, replica_groups=mesh['y'=8,'xh'=2,'core'=2,'xl'=2,'z'=8] {'xh','y'}, dimensions={0} | all-to-all | bytes 1048576 | tf_op jit(solution)/shard_map/all_to_all | solution.py:20
  72.9 0.1 reduce_sum.37
  73.0 0.1 broadcast_in_dim.7
  73.1 19.9 %all_to_all.32 = bf16[16,16,1024]{2,1,0:T(8,128)(2,1)S(1)} all-to-all(bf16[16,16,1024]{2,1,0:T(8,128)(2,1)S(1)} %broadcast_in_dim.7), channel_id=1, replica_groups=mesh['y'=8,'xh'=2,'core'=2,'xl'=2,'z'=8] {'xh','y'}, dimensions={0} | all-to-all | bytes 1048576 | tf_op jit(solution)/shard_map/all_to_all | solution.py:20
  92.9 0.2 fusion.3
  93.1 0.2 fusion.4
  93.4 0.7 pad_maximum_fusion.1
  94.1 7.6 %all-to-all-start.4 = ((bf16[16,16,512]{2,1,0:T(8,128)(2,1)}), bf16[16,16,512]{2,1,0:T(8,128)(2,1)S(1)}, u32[]{:S(2)}, u32[]{:S(2)}) async-start(bf16[16,16,512]{2,1,0:T(8,128)(2,1)} %pad_maximum_fusion.1), calls=%async_computation.4 | async-start | bytes 524288 | tf_op jit(solution)/shard_map/all_to_all | solution.py:20
  101.7 0.2 fusion.12
  101.9 0.0 copy-start.2
  102.0 0.2 fusion.9
  102.2 0.7 pad_maximum_fusion.2
  102.9 1.9 %collective-permute-start.3 = (f32[512,128]{1,0:T(8,128)}, f32[512,128]{1,0:T(8,128)}, u32[]{:S(2)}, u32[]{:S(2)}) collective-permute-start(f32[512,128]{1,0:T(8,128)} %pad_maximum_fusion.2), channel_id=1, source_target_pairs={{0,16},{16,0},{1,17},{17,1},{2,18},{18,2},{3,19},{19,3},{4,20},{20... | collective-permute-start | bytes 786440 | tf_op jit(solution)/shard_map/ppermute | solution.py:36
  104.8 5.9 %all-to-all-done.4 = bf16[16,16,512]{2,1,0:T(8,128)(2,1)S(1)} async-done(((bf16[16,16,512]{2,1,0:T(8,128)(2,1)}), bf16[16,16,512]{2,1,0:T(8,128)(2,1)S(1)}, u32[]{:S(2)}, u32[]{:S(2)}) %all-to-all-start.4) | async-done | bytes 262176 | tf_op jit(solution)/shard_map/all_to_all | solution.py:20
  110.8 1.9 %collective-permute-start.2 = (bf16[8,512]{1,0:T(8,128)(2,1)S(1)}, bf16[8,512]{1,0:T(8,128)(2,1)S(1)}, u32[]{:S(2)}, u32[]{:S(2)}) collective-permute-start(bf16[8,512]{1,0:T(8,128)(2,1)S(1)} %get-tuple-element.34), channel_id=1, source_target_pairs={{0,16},{16,0},{1,17},{17,1},{2,18},{18,2},{3,19},{19,3},{4,20},{20... | collective-permute-start | bytes 24584 | tf_op jit(solution)/shard_map/ppermute | solution.py:36
  112.7 1.1 collective-permute-done.2
  113.8 0.7 broadcast_in_dim.8
  114.6 4.2 %all-to-all-start.5 = ((bf16[16,8,1024]{2,1,0:T(8,128)(2,1)}), bf16[16,8,1024]{2,1,0:T(8,128)(2,1)S(1)}, u32[]{:S(2)}, u32[]{:S(2)}) async-start(bf16[16,8,1024]{2,1,0:T(8,128)(2,1)} %broadcast_in_dim.8), calls=%async_computation.5 | async-start | bytes 524288 | tf_op jit(solution)/shard_map/all_to_all | solution.py:20
  118.8 0.0 collective-permute-done.3
  118.8 0.9 fusion.20
  119.7 0.9 fusion.7
  120.5 1.8 %slice_add_fusion = f32[256,128]{1,0:T(8,128)} fusion(f32[512,128]{1,0:T(8,128)} %collective-permute-done.3, bf16[256,512]{1,0:T(8,128)(2,1)S(1)} %get-tuple-element.26, bf16[16,32,512]{2,1,0:T(8,128)(2,1)S(1)} %all_to_all.30), kind=kOutput, calls=%fused_computation.17 | convolution fusion | flops 33587200 | bytes 655360 | tf_op jit(solution)/shard_map/dot_general | solution.py:16
  122.3 7.0 %all-to-all-done.5 = bf16[16,8,1024]{2,1,0:T(8,128)(2,1)S(1)} async-done(((bf16[16,8,1024]{2,1,0:T(8,128)(2,1)}), bf16[16,8,1024]{2,1,0:T(8,128)(2,1)S(1)}, u32[]{:S(2)}, u32[]{:S(2)}) %all-to-all-start.5) | async-done | bytes 262176 | tf_op jit(solution)/shard_map/all_to_all | solution.py:20
  129.3 0.0 copy-done.2
  129.3 1.9 %fusion.5 = bf16[128,256]{1,0:T(8,128)(2,1)} fusion(bf16[1024,256]{1,0:T(8,128)(2,1)} %param.10, bf16[16,8,1024]{2,1,0:T(8,128)(2,1)S(1)} %all-to-all-done.5, bf16[128,256]{1,0:T(8,128)(2,1)S(1)} %copy-done.2), kind=kOutput, calls=%fused_computation.12 | convolution fusion | flops 67207168 | bytes 917504 | tf_op jit(solution)/shard_map/dot_general | solution.py:16
  (9 shorter events, 0.2 us)
Async XLA Ops:
  0.6 47.6 %copy-start = (bf16[256,4096]{1,0:T(8,128)(2,1)S(1)}, bf16[256,4096]{1,0:T(8,128)(2,1)}, u32[]{:S(2)}) copy-start(bf16[256,4096]{1,0:T(8,128)(2,1)} %param.8) | copy-start | bytes 6291460
  0.6 47.1 %copy-start.1 = (bf16[128,256]{1,0:T(8,128)(2,1)S(1)}, bf16[128,256]{1,0:T(8,128)(2,1)}, u32[]{:S(2)}) copy-start(bf16[128,256]{1,0:T(8,128)(2,1)} %param.6) | copy-start | bytes 196612
  2.9 21.5 %all-to-all-start = ((bf16[16,8,1024]{2,1,0:T(8,128)(2,1)}), bf16[16,8,1024]{2,1,0:T(8,128)(2,1)S(1)}, u32[]{:S(2)}, u32[]{:S(2)}) async-start(bf16[16,8,1024]{2,1,0:T(8,128)(2,1)} %fusion.2), calls=%async_computation | async-start | bytes 524288 | tf_op jit(solution)/shard_map/all_to_all | solution.py:20
  14.3 3.4 %collective-permute-start = (bf16[128,256]{1,0:T(8,128)(2,1)}, bf16[128,256]{1,0:T(8,128)(2,1)S(1)}, u32[]{:S(2)}, u32[]{:S(2)}) collective-permute-start(bf16[128,256]{1,0:T(8,128)(2,1)} %param.6), channel_id=1, source_target_pairs={{0,16},{16,0},{1,17},{17,1},{2,18},{18,2},{3,19},{19,3},{4,20},{20... | collective-permute-start | bytes 196616 | tf_op jit(solution)/shard_map/ppermute | solution.py:36
  24.5 3.1 %collective-permute-start.1 = (bf16[16,512]{1,0:T(8,128)(2,1)S(1)}, bf16[16,512]{1,0:T(8,128)(2,1)S(1)}, u32[]{:S(2)}, u32[]{:S(2)}) collective-permute-start(bf16[16,512]{1,0:T(8,128)(2,1)S(1)} %pad_maximum_fusion.4), channel_id=1, source_target_pairs={{0,16},{16,0},{1,17},{17,1},{2,18},{18,2},{3,19},{19,3},{4,20},{20... | collective-permute-start | bytes 49160 | tf_op jit(solution)/shard_map/ppermute | solution.py:36
  94.1 16.6 %all-to-all-start.4 = ((bf16[16,16,512]{2,1,0:T(8,128)(2,1)}), bf16[16,16,512]{2,1,0:T(8,128)(2,1)S(1)}, u32[]{:S(2)}, u32[]{:S(2)}) async-start(bf16[16,16,512]{2,1,0:T(8,128)(2,1)} %pad_maximum_fusion.1), calls=%async_computation.4 | async-start | bytes 524288 | tf_op jit(solution)/shard_map/all_to_all | solution.py:20
  101.9 27.4 %copy-start.2 = (bf16[128,256]{1,0:T(8,128)(2,1)S(1)}, bf16[128,256]{1,0:T(8,128)(2,1)}, u32[]{:S(2)}) copy-start(bf16[128,256]{1,0:T(8,128)(2,1)} %param.7) | copy-start | bytes 196612
  102.9 15.9 %collective-permute-start.3 = (f32[512,128]{1,0:T(8,128)}, f32[512,128]{1,0:T(8,128)}, u32[]{:S(2)}, u32[]{:S(2)}) collective-permute-start(f32[512,128]{1,0:T(8,128)} %pad_maximum_fusion.2), channel_id=1, source_target_pairs={{0,16},{16,0},{1,17},{17,1},{2,18},{18,2},{3,19},{19,3},{4,20},{20... | collective-permute-start | bytes 786440 | tf_op jit(solution)/shard_map/ppermute | solution.py:36
  110.8 3.1 %collective-permute-start.2 = (bf16[8,512]{1,0:T(8,128)(2,1)S(1)}, bf16[8,512]{1,0:T(8,128)(2,1)S(1)}, u32[]{:S(2)}, u32[]{:S(2)}) collective-permute-start(bf16[8,512]{1,0:T(8,128)(2,1)S(1)} %get-tuple-element.34), channel_id=1, source_target_pairs={{0,16},{16,0},{1,17},{17,1},{2,18},{18,2},{3,19},{19,3},{4,20},{20... | collective-permute-start | bytes 24584 | tf_op jit(solution)/shard_map/ppermute | solution.py:36
  114.6 14.7 %all-to-all-start.5 = ((bf16[16,8,1024]{2,1,0:T(8,128)(2,1)}), bf16[16,8,1024]{2,1,0:T(8,128)(2,1)S(1)}, u32[]{:S(2)}, u32[]{:S(2)}) async-start(bf16[16,8,1024]{2,1,0:T(8,128)(2,1)} %broadcast_in_dim.8), calls=%async_computation.5 | async-start | bytes 524288 | tf_op jit(solution)/shard_map/all_to_all | solution.py:20
